TPU v7x, 256 devices: a whole 4x4x8 slice. The times are simulated.
256 devices in a mesh: gy: 32 (over z_hi, y, x), gz: 8 (over z_lo, core).
Axes of the slice: x: 4, y: 4, z: 8 (z_hi: 2, z_lo: 4; z = z_hi * 4 + z_lo), core: 2. Of those that a mesh axis runs over, the one named last changes fastest.
Arguments:
- kspace: float32 [2, 4, 256, 32, 256], P(None, None, 'gy', 'gz'), may hold values from -6 to 6
- cotangent: float32 [2, 4, 256, 32, 256], P(None, None, 'gy', 'gz'), may hold values from -6 to 6
- weight_in: bfloat16 [16, 8, 3, 3, 3], replicated, may hold values from -0.4375 to 0.4375
- weight_out: bfloat16 [8, 16, 3, 3, 3], replicated, may hold values from -0.3125 to 0.3125
- consistency_weight: float32 [1], replicated, may hold values from 0.2 to 1
- sampling_mask: int32 [256, 32], P('gy', 'gz'), may hold values 0 or 1
Outputs:
- grad_kspace: float32 [2, 4, 256, 32, 256], P(None, None, 'gy', 'gz')
- grad_weight_in: float32 [16, 8, 3, 3, 3], replicated
- grad_weight_out: float32 [8, 16, 3, 3, 3], replicated
Inputs may be any that keep to these rules, and one draw needn't show every extreme that they name: `sampling_mask`: 1 marks a sampled phase-encode line.
All inputs are finite; a program needn't handle non-finite values. No bound on the sum of `sampling_mask` on one device may be relied on, other than what follows from the above.
Results may differ from a plain program's by a relative error of at most 0.0059.
Values may be sent and summed in bfloat16 or wider, within the bound.
A program may use at most 128 MiB of HBM per device.

v0:
```python
import math
import jax
import jax.numpy as jnp
from jax import lax
from jax.sharding import PartitionSpec as P


def as_sent(shard):
    return jax.tree.map(lambda a: a.astype(jnp.bfloat16) if a.dtype == jnp.float32 else a, shard)


def extended(shard, sides, width):
    for axis, dim in sides:
        count, length = (lax.axis_size(axis), shard.shape[dim])
        up = [(i, (i + 1) % count) for i in range(count - 1)]
        down = [(j, i) for i, j in up]
        last = lax.slice_in_dim(shard, length - width, length, axis=dim)
        first = lax.slice_in_dim(shard, 0, width, axis=dim)
        before = lax.ppermute(last, axis, up)
        after = lax.ppermute(first, axis, down)
        shard = jnp.concatenate([before, shard, after], axis=dim)
    return shard


def dft_table(length, direction):
    indices = lax.iota(jnp.int32, length)
    products = indices[:, None] * indices[None, :] % length
    phases = products.astype(jnp.float32) * (2.0 * math.pi / length)
    cosine = jnp.cos(phases) / math.sqrt(length)
    sine_part = direction * jnp.sin(phases) / math.sqrt(length)
    return jnp.stack([jnp.stack([cosine, -sine_part]), jnp.stack([sine_part, cosine])])


def spectral(spectrum, direction):
    field_parts = spectrum.shape[1]
    cells_y = spectrum.shape[2]
    cells_z = spectrum.shape[3]
    readout = spectrum.shape[4]
    length_y = cells_y * lax.axis_size("gy")
    length_z = cells_z * lax.axis_size("gz")
    table_y = dft_table(length_y, direction)
    table_z = dft_table(length_z, direction)
    flattened = spectrum.reshape(2, field_parts, cells_y, cells_z * readout)
    transformed_y = jnp.einsum(
        "pqvy,qcym->pcvm",
        table_y,
        lax.all_to_all(flattened, "gy", split_axis=3, concat_axis=2, tiled=True),
        precision=lax.Precision.HIGHEST,
    )
    turned_field = lax.all_to_all(
        lax.all_to_all(transformed_y, "gy", split_axis=2, concat_axis=3, tiled=True),
        "gz",
        split_axis=2,
        concat_axis=3,
        tiled=True,
    )
    shaped = turned_field.reshape(
        turned_field.shape[0], turned_field.shape[1], turned_field.shape[2], length_z, readout
    )
    turned = jnp.einsum("pqwz,qcyzx->pcywx", table_z, shaped, precision=lax.Precision.HIGHEST)
    transformed_z = turned.reshape(turned_field.shape)
    result = lax.all_to_all(
        as_sent(transformed_z), "gz", split_axis=3, concat_axis=2, tiled=True
    ).astype(transformed_z.dtype)
    return result.reshape(spectrum.shape)


def with_rims(volume):
    return extended(volume, (("gy", 2), ("gz", 3)), 1)


def convolve(padded, kernel):
    return lax.conv_general_dilated(
        padded,
        kernel,
        (1, 1, 1),
        ((0, 0), (0, 0), (1, 1)),
        dimension_numbers=("NCDHW", "OIDHW", "NCDHW"),
        preferred_element_type=jnp.float32,
    )


def kernel_gradient(padded, cotangent_part):
    summed = lax.conv_general_dilated(
        padded,
        cotangent_part,
        (1, 1, 1),
        ((0, 0), (0, 0), (1, 1)),
        dimension_numbers=("CNDHW", "IODHW", "NCDHW"),
        preferred_element_type=jnp.float32,
    )
    return summed.transpose(1, 0, 2, 3, 4)


def flipped(kernel):
    return jnp.flip(kernel, (2, 3, 4)).transpose(1, 0, 2, 3, 4)


def local(kspace, cotangent, weight_in, weight_out, consistency_weight, sampling_mask):
    coil_count = kspace.shape[1]
    channels = 2 * coil_count
    cells_y = kspace.shape[2]
    cells_z = kspace.shape[3]
    readout = kspace.shape[4]
    voxels = readout * cells_y * cells_z * lax.axis_size("gy") * lax.axis_size("gz")
    image_field = spectral(kspace, 1.0)
    back_field = spectral(cotangent, 1.0)
    image_in = image_field.astype(jnp.bfloat16).reshape(1, channels, cells_y, cells_z, readout)
    back_out = (-back_field).astype(jnp.bfloat16).reshape(1, channels, cells_y, cells_z, readout)
    image_padded = with_rims(image_in)
    back_padded = with_rims(back_out)
    hidden = convolve(image_padded, weight_in)
    active = jax.nn.silu(hidden).astype(jnp.bfloat16)
    active_padded = with_rims(active)
    local_out = kernel_gradient(active_padded, back_out)
    back_active = convolve(back_padded, flipped(weight_out))
    gate = jax.nn.sigmoid(hidden)
    back_hidden = (back_active * gate * (1.0 + hidden * (1.0 - gate))).astype(jnp.bfloat16)
    local_in = kernel_gradient(image_padded, back_hidden)
    hidden_padded = with_rims(back_hidden)
    back_image = convolve(hidden_padded, flipped(weight_in))
    spectrum = spectral(back_image.reshape(2, coil_count, cells_y, cells_z, readout), -1.0)
    summed_in, summed_out = lax.psum((local_in, local_out), ("gy", "gz"))
    scale = 1.0 / math.sqrt(voxels)
    mask_field = sampling_mask.astype(jnp.float32)[None, None, :, :, None]
    grad_kspace = cotangent - consistency_weight[0] * mask_field * cotangent + spectrum
    return (grad_kspace, summed_in * scale, summed_out * scale)


def solution(mesh):
    placed = (
        P(None, None, "gy", "gz", None),
        P(None, None, "gy", "gz", None),
        P(),
        P(),
        P(),
        P("gy", "gz"),
    )
    return jax.shard_map(
        local,
        mesh=mesh,
        in_specs=placed,
        out_specs=(P(None, None, "gy", "gz", None), P(), P()),
        check_vma=False,
    )
```

profile of v0, /device:TPU:1, one launch (start us, length us, event | category | flops | bytes accessed | tf_op | source)
XLA Modules:
  0.0 722.7 jit_solution(2760864033944492216)
XLA Ops:
  12.1 14.5 %all-to-all-start.4 = ((f32[32,1,2048]{2,1,0:T(1,128)}), f32[32,1,2048]{2,1,0:T(1,128)S(1)}, u32[]{:S(2)}, u32[]{:S(2)}) async-start(f32[32,1,2048]{2,1,0:T(1,128)} %reshape.431), calls=%async_computation.4 | async-start | bytes 524288 | tf_op jit(solution)/shard_map/all_to_all | solution.py:47
  38.5 11.0 %all-to-all-start = ((f32[32,1,2048]{2,1,0:T(1,128)}), f32[32,1,2048]{2,1,0:T(1,128)S(1)}, u32[]{:S(2)}, u32[]{:S(2)}) async-start(f32[32,1,2048]{2,1,0:T(1,128)} %reshape.437), calls=%async_computation | async-start | bytes 524288 | tf_op jit(solution)/shard_map/all_to_all | solution.py:47
  68.4 12.0 %all-to-all-start.5 = ((f32[32,1,2048]{2,1,0:T(1,128)}), f32[32,1,2048]{2,1,0:T(1,128)S(1)}, u32[]{:S(2)}, u32[]{:S(2)}) async-start(f32[32,1,2048]{2,1,0:T(1,128)} %reshape.433), calls=%async_computation.5 | async-start | bytes 524288 | tf_op jit(solution)/shard_map/all_to_all | solution.py:51
  95.5 11.8 %all-to-all-start.1 = ((f32[32,1,2048]{2,1,0:T(1,128)}), f32[32,1,2048]{2,1,0:T(1,128)S(1)}, u32[]{:S(2)}, u32[]{:S(2)}) async-start(f32[32,1,2048]{2,1,0:T(1,128)} %reshape.439), calls=%async_computation.1 | async-start | bytes 524288 | tf_op jit(solution)/shard_map/all_to_all | solution.py:51
  110.7 8.5 %all-to-all-done.1 = f32[32,1,2048]{2,1,0:T(1,128)S(1)} async-done(((f32[32,1,2048]{2,1,0:T(1,128)}), f32[32,1,2048]{2,1,0:T(1,128)S(1)}, u32[]{:S(2)}, u32[]{:S(2)}) %all-to-all-start.1) | async-done | bytes 262176 | tf_op jit(solution)/shard_map/all_to_all | solution.py:51
  119.2 7.4 %all-to-all-start.6 = ((f32[2,4,8,1024]{3,1,0,2:T(4,128)}), f32[2,4,8,1024]{3,1,0,2:T(4,128)S(1)}, u32[]{:S(2)}, u32[]{:S(2)}) async-start(f32[2,4,8,1024]{3,1,0,2:T(4,128)} %reshape.424), calls=%async_computation.6 | async-start | bytes 524288 | tf_op jit(solution)/shard_map/all_to_all | solution.py:50
  146.6 9.3 %reshape.435 = bf16[8,2,4096]{2,1,0:T(2,128)(2,1)} reshape(bf16[8192,1,2,4]{3,2,1,0:T(2,128)(2,1)} %bitcast.299) | data formatting | bytes 262144
  167.4 9.3 %reshape.441 = bf16[8,2,4096]{2,1,0:T(2,128)(2,1)} reshape(bf16[8192,1,2,4]{3,2,1,0:T(2,128)(2,1)} %bitcast.300) | data formatting | bytes 262144
  182.5 10.0 %reshape.436 = bf16[8192,1,2,4]{3,2,1,0:T(2,128)(2,1)} reshape(bf16[8,2,4096]{2,1,0:T(2,128)(2,1)S(1)} %all-to-all-done.7) | data formatting | bytes 262144
  192.6 8.6 %copy.358 = bf16[2,4,1,8192]{3,1,0,2:T(4,128)(2,1)S(1)} copy(bf16[2,4,1,8192]{1,0,2,3:T(2,128)(2,1)} %bitcast.301) | data formatting | bytes 262144 | tf_op jit(solution)/shard_map/all_to_all | solution.py:62
  203.3 10.1 %reshape.442 = bf16[8192,1,2,4]{3,2,1,0:T(2,128)(2,1)} reshape(bf16[8,2,4096]{2,1,0:T(2,128)(2,1)S(1)} %all-to-all-done.3) | data formatting | bytes 262144
  213.4 8.6 %copy.344 = bf16[2,4,1,8192]{3,1,2,0:T(4,128)(2,1)S(1)} copy(bf16[2,4,1,8192]{1,0,2,3:T(2,128)(2,1)} %bitcast.302) | data formatting | bytes 262144 | tf_op jit(solution)/shard_map/all_to_all | solution.py:62
  269.0 9.1 %multiply_convert_fusion.1 = (bf16[8,4,8,33,16]{4,2,3,1,0:T(8,128)(2,1)}, f32[8,4,8,33,16]{4,2,3,1,0:T(8,128)S(1)}) fusion(pred[8,33]{0,1:T(8,128)(4,1)S(1)} %copy-done.15, bf16[16,8,3,3,3]{0,1,4,3,2:T(8,128)(2,1)S(1)} %copy-done, bf16[8,10,6,1,7,2]{0,4,5,2,1,3:T(8,128)(2,1)S(1)} %copy-done.8, bf16[8,10,6,1,8,33]{0,4,5,2,1,3:T(8,128)(2,1)} %copy.361), kind=kOutput, calls=%fused_computation.16 | convolution fusion | flops 60009984 | bytes 1085064 | tf_op jit(solution)/shard_map/conv_general_dilated | solution.py:73
  278.2 9.5 %multiply_convert_fusion = bf16[8,4,8,33,16]{4,2,3,1,0:T(8,128)(2,1)} fusion(f32[8,4,8,33,16]{4,2,3,1,0:T(8,128)S(1)} %get-tuple-element.36, bf16[8,16,3,3,3]{1,0,4,3,2:T(8,128)(2,1)S(1)} %copy-done.14, bf16[8,10,6,1,7,2]{0,4,5,2,1,3:T(8,128)(2,1)S(1)} %slice.86, bf16[8,10,6,1,8,33]{0,4,5,2,1,3:T(8,128)(2,1)S(1)} %copy-done.2, pred[8,33]{0,1:T(8,128)(4,1)S(1)} %copy-done.15), kind=kOutput, calls=%fused_computation.15 | convolution fusion | flops 60685824 | bytes 1085064 | tf_op jit(solution)/shard_map/conv_general_dilated | solution.py:73
  345.9 9.1 %broadcast_select_fusion = f32[8,4,8,33,8]{4,2,3,1,0:T(8,128)} fusion(pred[8,33]{0,1:T(8,128)(4,1)S(1)} %copy-done.15, bf16[16,8,3,3,3]{0,1,4,3,2:T(8,128)(2,1)S(1)} %copy-done, bf16[16,10,6,1,7,2]{0,4,5,2,1,3:T(8,128)(2,1)S(1)} %slice.97, bf16[16,10,6,1,8,33]{0,4,5,2,1,3:T(8,128)(2,1)} %copy.368), kind=kOutput, calls=%fused_computation.41 | convolution fusion | flops 60072960 | bytes 811272 | tf_op jit(solution)/shard_map/conv_general_dilated | solution.py:73
  368.4 37.0 %all-to-all-start.8 = ((f32[32,1,2048]{2,1,0:T(1,128)}), f32[32,1,2048]{2,1,0:T(1,128)S(1)}, u32[]{:S(2)}, u32[]{:S(2)}) async-start(f32[32,1,2048]{2,1,0:T(1,128)} %reshape.443), calls=%async_computation.8 | async-start | bytes 524288 | tf_op jit(solution)/shard_map/all_to_all | solution.py:47
  446.6 12.3 %all-to-all-start.9 = ((f32[32,1,2048]{2,1,0:T(1,128)}), f32[32,1,2048]{2,1,0:T(1,128)S(1)}, u32[]{:S(2)}, u32[]{:S(2)}) async-start(f32[32,1,2048]{2,1,0:T(1,128)} %reshape.445), calls=%async_computation.9 | async-start | bytes 524288 | tf_op jit(solution)/shard_map/all_to_all | solution.py:51
  458.9 22.9 %fusion.52 = f32[16,8,3,3,3]{0,1,4,3,2:T(8,128)} fusion(bf16[8,4,8,33,16]{4,2,3,1,0:T(8,128)(2,1)S(1)} %copy-done.5, pred[8,33]{0,1:T(8,128)(4,1)S(1)} %copy-done.15, bf16[8,10,6,8,33,1]{3,0,5,4,2,1:T(8,128)(2,1)} %fusion.33, bf16[8,10,6,8,33,1]{3,0,5,4,2,1:T(8,128)(2,1)} %copy.388, bf16[8,10,6,8,33,1]{3,0,5,4,2,1:T(8,128)(2,1)} %fusion.35), kind=kOutput, calls=%fused_computation.59 | convolution fusion | flops 59288064 | bytes 1044744 | tf_op jit(solution)/shard_map/transpose | solution.py:92
  482.8 12.0 %copy.395 = bf16[1,16,10,6,256]{1,0,4,3,2:T(2,128)(2,1)} copy(bf16[1,16,10,6,256]{4,1,3,2,0:T(8,128)(2,1)S(1)} %pad_maximum_fusion.7) | data formatting | bytes 983040 | tf_op jit(solution)/shard_map/concatenate | solution.py:21
  504.1 90.1 %fusion.123 = f32[8,16,3,3,3]{1,0,4,3,2:T(8,128)S(1)} fusion(bf16[1,16,10,6,256]{1,0,4,3,2:T(2,128)(2,1)} %copy.395, bf16[1,8,8,4,256]{1,0,4,3,2:T(2,128)(2,1)} %copy.396), kind=kOutput, calls=%fused_computation.182 | convolution fusion | flops 56475648 | bytes 636416 | tf_op jit(solution)/shard_map/transpose | solution.py:92
  594.2 82.3 %all-reduce = (f32[16,8,3,3,3]{0,1,4,3,2:T(8,128)S(1)}, f32[8,16,3,3,3]{1,0,4,3,2:T(8,128)S(1)}) all-reduce(f32[16,8,3,3,3]{0,1,4,3,2:T(8,128)S(1)} %copy-done.11, f32[8,16,3,3,3]{1,0,4,3,2:T(8,128)S(1)} %fusion.123), channel_id=1, replica_groups=mesh['gy'=32,'gz'=8] {'gy','gz'}, use_global_device_ids=true, to_apply=%region_0.1 | all-reduce | flops 6912 | bytes 55296 | tf_op jit(solution)/shard_map/psum | solution.py:123
  682.8 9.3 %reshape.447 = bf16[8,2,4096]{2,1,0:T(2,128)(2,1)} reshape(bf16[8192,1,2,4]{3,2,1,0:T(2,128)(2,1)} %bitcast.304) | data formatting | bytes 262144
  701.9 10.0 %reshape.448 = bf16[8192,1,2,4]{3,2,1,0:T(2,128)(2,1)} reshape(bf16[8,2,4096]{2,1,0:T(2,128)(2,1)S(1)} %all-to-all-done.11) | data formatting | bytes 262144
  712.0 9.6 %copy.381 = f32[2,4,8,4,256]{4,3,2,1,0:T(4,128)S(1)} copy(bf16[2,4,8,4,256]{1,0,4,3,2:T(2,128)(2,1)} %bitcast.305) | data formatting | bytes 393216 | tf_op jit(solution)/shard_map/convert_element_type | solution.py:64
  (212 shorter events, 285.7 us)
Async XLA Ops:
  12.1 26.5 %all-to-all-start.4 = ((f32[32,1,2048]{2,1,0:T(1,128)}), f32[32,1,2048]{2,1,0:T(1,128)S(1)}, u32[]{:S(2)}, u32[]{:S(2)}) async-start(f32[32,1,2048]{2,1,0:T(1,128)} %reshape.431), calls=%async_computation.4 | async-start | bytes 524288 | tf_op jit(solution)/shard_map/all_to_all | solution.py:47
  38.5 29.9 %all-to-all-start = ((f32[32,1,2048]{2,1,0:T(1,128)}), f32[32,1,2048]{2,1,0:T(1,128)S(1)}, u32[]{:S(2)}, u32[]{:S(2)}) async-start(f32[32,1,2048]{2,1,0:T(1,128)} %reshape.437), calls=%async_computation | async-start | bytes 524288 | tf_op jit(solution)/shard_map/all_to_all | solution.py:47
  68.4 27.1 %all-to-all-start.5 = ((f32[32,1,2048]{2,1,0:T(1,128)}), f32[32,1,2048]{2,1,0:T(1,128)S(1)}, u32[]{:S(2)}, u32[]{:S(2)}) async-start(f32[32,1,2048]{2,1,0:T(1,128)} %reshape.433), calls=%async_computation.5 | async-start | bytes 524288 | tf_op jit(solution)/shard_map/all_to_all | solution.py:51
  95.5 23.8 %all-to-all-start.1 = ((f32[32,1,2048]{2,1,0:T(1,128)}), f32[32,1,2048]{2,1,0:T(1,128)S(1)}, u32[]{:S(2)}, u32[]{:S(2)}) async-start(f32[32,1,2048]{2,1,0:T(1,128)} %reshape.439), calls=%async_computation.1 | async-start | bytes 524288 | tf_op jit(solution)/shard_map/all_to_all | solution.py:51
  119.2 16.2 %all-to-all-start.6 = ((f32[2,4,8,1024]{3,1,0,2:T(4,128)}), f32[2,4,8,1024]{3,1,0,2:T(4,128)S(1)}, u32[]{:S(2)}, u32[]{:S(2)}) async-start(f32[2,4,8,1024]{3,1,0,2:T(4,128)} %reshape.424), calls=%async_computation.6 | async-start | bytes 524288 | tf_op jit(solution)/shard_map/all_to_all | solution.py:50
  135.4 20.6 %all-to-all-start.2 = ((f32[2,4,8,1024]{3,1,0,2:T(4,128)}), f32[2,4,8,1024]{3,1,0,2:T(4,128)S(1)}, u32[]{:S(2)}, u32[]{:S(2)}) async-start(f32[2,4,8,1024]{3,1,0,2:T(4,128)} %reshape.422), calls=%async_computation.2 | async-start | bytes 524288 | tf_op jit(solution)/shard_map/all_to_all | solution.py:50
  156.0 20.8 %all-to-all-start.7 = ((bf16[8,2,4096]{2,1,0:T(2,128)(2,1)}), bf16[8,2,4096]{2,1,0:T(2,128)(2,1)S(1)}, u32[]{:S(2)}, u32[]{:S(2)}) async-start(bf16[8,2,4096]{2,1,0:T(2,128)(2,1)} %reshape.435), calls=%async_computation.7 | async-start | bytes 262144 | tf_op jit(solution)/shard_map/all_to_all | solution.py:62
  176.7 26.5 %all-to-all-start.3 = ((bf16[8,2,4096]{2,1,0:T(2,128)(2,1)}), bf16[8,2,4096]{2,1,0:T(2,128)(2,1)S(1)}, u32[]{:S(2)}, u32[]{:S(2)}) async-start(bf16[8,2,4096]{2,1,0:T(2,128)(2,1)} %reshape.441), calls=%async_computation.3 | async-start | bytes 262144 | tf_op jit(solution)/shard_map/all_to_all | solution.py:62
  201.4 34.8 %collective-permute-start.4 = (bf16[1,8,1,4,256]{4,3,2,1,0:T(4,128)(2,1)S(1)}, bf16[1,8,1,4,256]{4,3,2,1,0:T(4,128)(2,1)S(1)}, u32[]{:S(2)}, u32[]{:S(2)}) collective-permute-start(bf16[1,8,1,4,256]{4,3,2,1,0:T(4,128)(2,1)S(1)} %get-tuple-element.30), channel_id=1, source_target_pairs={{0,8},{8,16},{16,24},{24,32},{32,40},{40,48},{48,56},{56,64},{64,7... | collective-permute-start | bytes 49160 | tf_op jit(solution)/shard_map/ppermute | solution.py:19
  230.9 11.9 %collective-permute-start = (bf16[1,8,1,4,256]{4,3,2,1,0:T(4,128)(2,1)S(1)}, bf16[1,8,1,4,256]{4,3,2,1,0:T(4,128)(2,1)S(1)}, u32[]{:S(2)}, u32[]{:S(2)}) collective-permute-start(bf16[1,8,1,4,256]{4,3,2,1,0:T(4,128)(2,1)S(1)} %get-tuple-element.28), channel_id=1, source_target_pairs={{0,8},{8,16},{16,24},{24,32},{32,40},{40,48},{48,56},{56,64},{64,7... | collective-permute-start | bytes 49160 | tf_op jit(solution)/shard_map/ppermute | solution.py:19
  236.5 12.8 %collective-permute-start.6 = (bf16[1,8,10,1,256]{4,3,2,1,0:T(2,128)(2,1)S(1)}, bf16[1,8,10,1,256]{4,3,2,1,0:T(2,128)(2,1)S(1)}, u32[]{:S(2)}, u32[]{:S(2)}) collective-permute-start(bf16[1,8,10,1,256]{4,3,2,1,0:T(2,128)(2,1)S(1)} %get-tuple-element.25), channel_id=1, source_target_pairs={{0,1},{1,2},{2,3},{3,4},{4,5},{5,6},{6,7},{8,9},{9,10},{10,11},{11... | collective-permute-start | bytes 122888 | tf_op jit(solution)/shard_map/ppermute | solution.py:19
  243.7 17.3 %collective-permute-start.2 = (bf16[1,8,10,1,256]{4,3,2,1,0:T(2,128)(2,1)}, bf16[1,8,10,1,256]{4,3,2,1,0:T(2,128)(2,1)}, u32[]{:S(2)}, u32[]{:S(2)}) collective-permute-start(bf16[1,8,10,1,256]{4,3,2,1,0:T(2,128)(2,1)} %get-tuple-element.23), channel_id=1, source_target_pairs={{0,1},{1,2},{2,3},{3,4},{4,5},{5,6},{6,7},{8,9},{9,10},{10,11},{11... | collective-permute-start | bytes 122888 | tf_op jit(solution)/shard_map/ppermute | solution.py:19
  247.3 13.7 %collective-permute-start.3 = (bf16[1,8,10,1,256]{4,3,2,1,0:T(2,128)(2,1)}, bf16[1,8,10,1,256]{4,3,2,1,0:T(2,128)(2,1)}, u32[]{:S(2)}, u32[]{:S(2)}) collective-permute-start(bf16[1,8,10,1,256]{4,3,2,1,0:T(2,128)(2,1)} %get-tuple-element.24), channel_id=1, source_target_pairs={{1,0},{2,1},{3,2},{4,3},{5,4},{6,5},{7,6},{9,8},{10,9},{11,10},{12... | collective-permute-start | bytes 122888 | tf_op jit(solution)/shard_map/ppermute | solution.py:20
  296.9 122.3 %collective-permute-start.12 = (bf16[1,16,1,4,256]{4,1,3,0,2:T(8,128)(2,1)}, bf16[1,16,1,4,256]{4,1,3,0,2:T(8,128)(2,1)}, u32[]{:S(2)}, u32[]{:S(2)}) collective-permute-start(bf16[1,16,1,4,256]{4,1,3,0,2:T(8,128)(2,1)} %slice_bitcast_fusion.4), channel_id=1, source_target_pairs={{0,8},{8,16},{16,24},{24,32},{32,40},{40,48},{48,56},{56,64},{64,7... | collective-permute-start | bytes 98312 | tf_op jit(solution)/shard_map/ppermute | solution.py:19
  303.2 116.0 %collective-permute-start.13 = (bf16[1,16,1,4,256]{4,1,3,0,2:T(8,128)(2,1)}, bf16[1,16,1,4,256]{4,1,3,0,2:T(8,128)(2,1)}, u32[]{:S(2)}, u32[]{:S(2)}) collective-permute-start(bf16[1,16,1,4,256]{4,1,3,0,2:T(8,128)(2,1)} %slice_bitcast_fusion.3), channel_id=1, source_target_pairs={{8,0},{16,8},{24,16},{32,24},{40,32},{48,40},{56,48},{64,56},{72,6... | collective-permute-start | bytes 98312 | tf_op jit(solution)/shard_map/ppermute | solution.py:20
  306.7 13.5 %collective-permute-start.8 = (bf16[1,16,1,4,256]{4,1,3,0,2:T(8,128)(2,1)S(1)}, bf16[1,16,1,4,256]{4,1,3,0,2:T(8,128)(2,1)S(1)}, u32[]{:S(2)}, u32[]{:S(2)}) collective-permute-start(bf16[1,16,1,4,256]{4,1,3,0,2:T(8,128)(2,1)S(1)} %slice_bitcast_fusion.6), channel_id=1, source_target_pairs={{0,8},{8,16},{16,24},{24,32},{32,40},{40,48},{48,56},{56,64},{64,7... | collective-permute-start | bytes 98312 | tf_op jit(solution)/shard_map/ppermute | solution.py:19
  320.3 16.8 %collective-permute-start.10 = (bf16[1,16,10,1,256]{4,1,3,2,0:T(8,128)(2,1)S(1)}, bf16[1,16,10,1,256]{4,1,3,2,0:T(8,128)(2,1)S(1)}, u32[]{:S(2)}, u32[]{:S(2)}) collective-permute-start(bf16[1,16,10,1,256]{4,1,3,2,0:T(8,128)(2,1)S(1)} %get-tuple-element.17), channel_id=1, source_target_pairs={{0,1},{1,2},{2,3},{3,4},{4,5},{5,6},{6,7},{8,9},{9,10},{10,11},{11... | collective-permute-start | bytes 245768 | tf_op jit(solution)/shard_map/ppermute | solution.py:19
  324.8 12.3 %collective-permute-start.11 = (bf16[1,16,10,1,256]{4,1,3,2,0:T(8,128)(2,1)S(1)}, bf16[1,16,10,1,256]{4,1,3,2,0:T(8,128)(2,1)}, u32[]{:S(2)}, u32[]{:S(2)}) collective-permute-start(bf16[1,16,10,1,256]{4,1,3,2,0:T(8,128)(2,1)S(1)} %get-tuple-element.18), channel_id=1, source_target_pairs={{1,0},{2,1},{3,2},{4,3},{5,4},{6,5},{7,6},{9,8},{10,9},{11,10},{12... | collective-permute-start | bytes 245768 | tf_op jit(solution)/shard_map/ppermute | solution.py:20
  368.4 58.1 %all-to-all-start.8 = ((f32[32,1,2048]{2,1,0:T(1,128)}), f32[32,1,2048]{2,1,0:T(1,128)S(1)}, u32[]{:S(2)}, u32[]{:S(2)}) async-start(f32[32,1,2048]{2,1,0:T(1,128)} %reshape.443), calls=%async_computation.8 | async-start | bytes 524288 | tf_op jit(solution)/shard_map/all_to_all | solution.py:47
  420.6 61.2 %collective-permute-start.14 = (bf16[1,16,10,1,256]{4,1,3,2,0:T(8,128)(2,1)}, bf16[1,16,10,1,256]{4,1,3,2,0:T(8,128)(2,1)}, u32[]{:S(2)}, u32[]{:S(2)}) collective-permute-start(bf16[1,16,10,1,256]{4,1,3,2,0:T(8,128)(2,1)} %get-tuple-element.13), channel_id=1, source_target_pairs={{0,1},{1,2},{2,3},{3,4},{4,5},{5,6},{6,7},{8,9},{9,10},{10,11},{11... | collective-permute-start | bytes 245768 | tf_op jit(solution)/shard_map/ppermute | solution.py:19
  424.5 57.3 %collective-permute-start.15 = (bf16[1,16,10,1,256]{4,1,3,2,0:T(8,128)(2,1)}, bf16[1,16,10,1,256]{4,1,3,2,0:T(8,128)(2,1)}, u32[]{:S(2)}, u32[]{:S(2)}) collective-permute-start(bf16[1,16,10,1,256]{4,1,3,2,0:T(8,128)(2,1)} %get-tuple-element.14), channel_id=1, source_target_pairs={{1,0},{2,1},{3,2},{4,3},{5,4},{6,5},{7,6},{9,8},{10,9},{11,10},{12... | collective-permute-start | bytes 245768 | tf_op jit(solution)/shard_map/ppermute | solution.py:20
  446.6 48.2 %all-to-all-start.9 = ((f32[32,1,2048]{2,1,0:T(1,128)}), f32[32,1,2048]{2,1,0:T(1,128)S(1)}, u32[]{:S(2)}, u32[]{:S(2)}) async-start(f32[32,1,2048]{2,1,0:T(1,128)} %reshape.445), calls=%async_computation.9 | async-start | bytes 524288 | tf_op jit(solution)/shard_map/all_to_all | solution.py:51
  498.6 178.5 %all-to-all-start.10 = ((f32[2,4,8,1024]{3,1,0,2:T(4,128)}), f32[2,4,8,1024]{3,1,0,2:T(4,128)S(1)}, u32[]{:S(2)}, u32[]{:S(2)}) async-start(f32[2,4,8,1024]{3,1,0,2:T(4,128)} %reshape.426), calls=%async_computation.10 | async-start | bytes 524288 | tf_op jit(solution)/shard_map/all_to_all | solution.py:50
  692.1 9.8 %all-to-all-start.11 = ((bf16[8,2,4096]{2,1,0:T(2,128)(2,1)}), bf16[8,2,4096]{2,1,0:T(2,128)(2,1)S(1)}, u32[]{:S(2)}, u32[]{:S(2)}) async-start(bf16[8,2,4096]{2,1,0:T(2,128)(2,1)} %reshape.447), calls=%async_computation.11 | async-start | bytes 262144 | tf_op jit(solution)/shard_map/all_to_all | solution.py:62
  (20 other events, 932.0 us)
where the time goes:
time: 732 us; the launch traced here: 723 us
  local copies, waits for them, and re-layouts  264 us (36%)
  starting transfers between devices  175 us (24%)
  matrix products  151 us (21%)
  blocking collectives  82.3 us (11%)
  other arithmetic  28 us (4%)
  waiting for transfers between devices  19.7 us (3%)
    unnamed x60, local copies, waits for them, and re-layouts  126 us
    transpose x2, matrix products, kernel_gradient(): return summed.transpose(1, 0, 2, 3, 4)  113 us
    psum x1, blocking collectives, local(): summed_in, summed_out = lax.psum((local_in, local_out), ('gy', 'gz'))  82.3 us
    all_to_all x3, starting transfers between devices, spectral(): lax.all_to_all(flattened, 'gy', split_axis=3, concat_axis=2, tiled=True)  62.5 us
    all_to_all x3, starting transfers between devices, spectral(): lax.all_to_all(transformed_y, 'gy', split_axis=2, concat_axis=3, tiled=True)  36.1 us
    ppermute x8, starting transfers between devices, extended(): before = lax.ppermute(last, axis, up)  31.5 us
    conv_general_dilated x3, matrix products, convolve(): lax.conv_general_dilated(padded, kernel, (1, 1, 1), ((0, 0), (0, 0), (1,...  27.8 us
    conv_general_dilated x12, local copies, waits for them, and re-layouts, convolve(): lax.conv_general_dilated(padded, kernel, (1, 1, 1), ((0, 0), (0, 0), (1,...  25.1 us
  transfers between devices with their start and end apart: 28, of which 4 were waited for; matrix products, arithmetic and copies ran while one was open for 49% of the time, Pallas kernels for 0%

commit v1 on v0

--- a/solution.py
+++ b/solution.py
@@ -120,7 +120,7 @@
     hidden_padded = with_rims(back_hidden)
     back_image = convolve(hidden_padded, flipped(weight_in))
     spectrum = spectral(back_image.reshape(2, coil_count, cells_y, cells_z, readout), -1.0)
-    summed_in, summed_out = lax.psum((local_in, local_out), ("gy", "gz"))
+    summed_in, summed_out = jax.lax.psum(jax.lax.psum((local_in, local_out), "gz"), "gy")
     scale = 1.0 / math.sqrt(voxels)
     mask_field = sampling_mask.astype(jnp.float32)[None, None, :, :, None]
     grad_kspace = cotangent - consistency_weight[0] * mask_field * cotangent + spectrum

time: 732 us -> 906 us (1.24)
  blocking collectives: 82.3 us -> 227 us
  starting transfers between devices: 175 us -> 206 us
    psum x1 -> x2, blocking collectives: 82.3 us -> 227 us  [the longest x1 199 us: local(): jax.lax.psum(jax.lax.psum((local_in, local_out), 'gz'), 'gy')]
    all_to_all x3, starting transfers between devices: 14.2 us -> 45.1 us  [spectral(): lax.all_to_all(as_sent(transformed_z), 'gz', split_axis=3, concat_axis=2,...]
  transfers between devices with their start and end apart: 28 -> 28, of which waited for: 4 -> 4; matrix products, arithmetic and copies ran while one was open for 49% -> 40% of each run, Pallas kernels for 0% -> 0%
where the time goes in v1:
time: 906 us; the launch traced here: 898 us
  local copies, waits for them, and re-layouts  264 us (29%)
  blocking collectives  227 us (25%)
  starting transfers between devices  206 us (23%)
  matrix products  152 us (17%)
  other arithmetic  27.7 us (3%)
  waiting for transfers between devices  19.8 us (2%)
    psum x1, blocking collectives, local(): jax.lax.psum(jax.lax.psum((local_in, local_out), 'gz'), 'gy')  199 us
    unnamed x60, local copies, waits for them, and re-layouts  126 us
    transpose x2, matrix products, kernel_gradient(): return summed.transpose(1, 0, 2, 3, 4)  113 us
    all_to_all x3, starting transfers between devices, spectral(): lax.all_to_all(flattened, 'gy', split_axis=3, concat_axis=2, tiled=True)  62.5 us
    all_to_all x3, starting transfers between devices, spectral(): lax.all_to_all(as_sent(transformed_z), 'gz', split_axis=3, concat_axis=2,...  45.1 us
    all_to_all x3, starting transfers between devices, spectral(): lax.all_to_all(transformed_y, 'gy', split_axis=2, concat_axis=3, tiled=True)  36.1 us
    ppermute x8, starting transfers between devices, extended(): before = lax.ppermute(last, axis, up)  31.5 us
    psum x1, blocking collectives, local(): jax.lax.psum((local_in, local_out), 'gz')  27.9 us
  transfers between devices with their start and end apart: 28, of which 4 were waited for; matrix products, arithmetic and copies ran while one was open for 40% of the time, Pallas kernels for 0%

profile of v1, /device:TPU:1, one launch (start us, length us, event | category | flops | bytes accessed | tf_op | source)
XLA Modules:
  0.0 897.6 jit_solution(4311568694224994343)
XLA Ops:
  12.0 14.5 %all-to-all-start.4 = ((f32[32,1,2048]{2,1,0:T(1,128)}), f32[32,1,2048]{2,1,0:T(1,128)S(1)}, u32[]{:S(2)}, u32[]{:S(2)}) async-start(f32[32,1,2048]{2,1,0:T(1,128)} %reshape.431), calls=%async_computation.4 | async-start | bytes 524288 | tf_op jit(solution)/shard_map/all_to_all | solution.py:47
  38.5 11.0 %all-to-all-start = ((f32[32,1,2048]{2,1,0:T(1,128)}), f32[32,1,2048]{2,1,0:T(1,128)S(1)}, u32[]{:S(2)}, u32[]{:S(2)}) async-start(f32[32,1,2048]{2,1,0:T(1,128)} %reshape.437), calls=%async_computation | async-start | bytes 524288 | tf_op jit(solution)/shard_map/all_to_all | solution.py:47
  68.3 12.0 %all-to-all-start.5 = ((f32[32,1,2048]{2,1,0:T(1,128)}), f32[32,1,2048]{2,1,0:T(1,128)S(1)}, u32[]{:S(2)}, u32[]{:S(2)}) async-start(f32[32,1,2048]{2,1,0:T(1,128)} %reshape.433), calls=%async_computation.5 | async-start | bytes 524288 | tf_op jit(solution)/shard_map/all_to_all | solution.py:51
  95.3 11.8 %all-to-all-start.1 = ((f32[32,1,2048]{2,1,0:T(1,128)}), f32[32,1,2048]{2,1,0:T(1,128)S(1)}, u32[]{:S(2)}, u32[]{:S(2)}) async-start(f32[32,1,2048]{2,1,0:T(1,128)} %reshape.439), calls=%async_computation.1 | async-start | bytes 524288 | tf_op jit(solution)/shard_map/all_to_all | solution.py:51
  146.4 9.3 %reshape.435 = bf16[8,2,4096]{2,1,0:T(2,128)(2,1)} reshape(bf16[8192,1,2,4]{3,2,1,0:T(2,128)(2,1)} %bitcast.299) | data formatting | bytes 262144
  167.1 9.3 %reshape.441 = bf16[8,2,4096]{2,1,0:T(2,128)(2,1)} reshape(bf16[8192,1,2,4]{3,2,1,0:T(2,128)(2,1)} %bitcast.300) | data formatting | bytes 262144
  182.3 10.0 %reshape.436 = bf16[8192,1,2,4]{3,2,1,0:T(2,128)(2,1)} reshape(bf16[8,2,4096]{2,1,0:T(2,128)(2,1)S(1)} %all-to-all-done.7) | data formatting | bytes 262144
  192.3 8.6 copy.358
  203.0 10.0 %reshape.442 = bf16[8192,1,2,4]{3,2,1,0:T(2,128)(2,1)} reshape(bf16[8,2,4096]{2,1,0:T(2,128)(2,1)S(1)} %all-to-all-done.3) | data formatting | bytes 262144
  213.0 8.6 copy.344
  268.7 9.1 %multiply_convert_fusion.1 = (bf16[8,4,8,33,16]{4,2,3,1,0:T(8,128)(2,1)}, f32[8,4,8,33,16]{4,2,3,1,0:T(8,128)S(1)}) fusion(pred[8,33]{0,1:T(8,128)(4,1)S(1)} %copy-done.15, bf16[16,8,3,3,3]{0,1,4,3,2:T(8,128)(2,1)S(1)} %copy-done, bf16[8,10,6,1,7,2]{0,4,5,2,1,3:T(8,128)(2,1)S(1)} %copy-done.8, bf16[8,10,6,1,8,33]{0,4,5,2,1,3:T(8,128)(2,1)} %copy.361), kind=kOutput, calls=%fused_computation.16 | convolution fusion | flops 60009984 | bytes 1085064 | tf_op jit(solution)/shard_map/conv_general_dilated | solution.py:73
  277.8 9.5 %multiply_convert_fusion = bf16[8,4,8,33,16]{4,2,3,1,0:T(8,128)(2,1)} fusion(f32[8,4,8,33,16]{4,2,3,1,0:T(8,128)S(1)} %get-tuple-element.38, bf16[8,16,3,3,3]{1,0,4,3,2:T(8,128)(2,1)S(1)} %copy-done.14, bf16[8,10,6,1,7,2]{0,4,5,2,1,3:T(8,128)(2,1)S(1)} %slice.86, bf16[8,10,6,1,8,33]{0,4,5,2,1,3:T(8,128)(2,1)S(1)} %copy-done.2, pred[8,33]{0,1:T(8,128)(4,1)S(1)} %copy-done.15), kind=kOutput, calls=%fused_computation.15 | convolution fusion | flops 60685824 | bytes 1085064 | tf_op jit(solution)/shard_map/conv_general_dilated | solution.py:73
  345.6 9.1 %broadcast_select_fusion = f32[8,4,8,33,8]{4,2,3,1,0:T(8,128)} fusion(pred[8,33]{0,1:T(8,128)(4,1)S(1)} %copy-done.15, bf16[16,8,3,3,3]{0,1,4,3,2:T(8,128)(2,1)S(1)} %copy-done, bf16[16,10,6,1,7,2]{0,4,5,2,1,3:T(8,128)(2,1)S(1)} %slice.97, bf16[16,10,6,1,8,33]{0,4,5,2,1,3:T(8,128)(2,1)} %copy.368), kind=kOutput, calls=%fused_computation.41 | convolution fusion | flops 60072960 | bytes 811272 | tf_op jit(solution)/shard_map/conv_general_dilated | solution.py:73
  368.1 37.0 %all-to-all-start.8 = ((f32[32,1,2048]{2,1,0:T(1,128)}), f32[32,1,2048]{2,1,0:T(1,128)S(1)}, u32[]{:S(2)}, u32[]{:S(2)}) async-start(f32[32,1,2048]{2,1,0:T(1,128)} %reshape.443), calls=%async_computation.8 | async-start | bytes 524288 | tf_op jit(solution)/shard_map/all_to_all | solution.py:47
  446.3 12.3 %all-to-all-start.9 = ((f32[32,1,2048]{2,1,0:T(1,128)}), f32[32,1,2048]{2,1,0:T(1,128)S(1)}, u32[]{:S(2)}, u32[]{:S(2)}) async-start(f32[32,1,2048]{2,1,0:T(1,128)} %reshape.445), calls=%async_computation.9 | async-start | bytes 524288 | tf_op jit(solution)/shard_map/all_to_all | solution.py:51
  458.6 22.9 %fusion.52 = f32[16,8,3,3,3]{0,1,4,3,2:T(8,128)} fusion(bf16[8,4,8,33,16]{4,2,3,1,0:T(8,128)(2,1)S(1)} %copy-done.5, pred[8,33]{0,1:T(8,128)(4,1)S(1)} %copy-done.15, bf16[8,10,6,8,33,1]{3,0,5,4,2,1:T(8,128)(2,1)} %fusion.33, bf16[8,10,6,8,33,1]{3,0,5,4,2,1:T(8,128)(2,1)} %copy.388, bf16[8,10,6,8,33,1]{3,0,5,4,2,1:T(8,128)(2,1)} %fusion.35), kind=kOutput, calls=%fused_computation.59 | convolution fusion | flops 59288064 | bytes 1044744 | tf_op jit(solution)/shard_map/transpose | solution.py:92
  482.5 11.9 %copy.395 = bf16[1,16,10,6,256]{1,0,4,3,2:T(2,128)(2,1)} copy(bf16[1,16,10,6,256]{4,1,3,2,0:T(8,128)(2,1)S(1)} %pad_maximum_fusion.7) | data formatting | bytes 983040 | tf_op jit(solution)/shard_map/concatenate | solution.py:21
  503.7 90.1 %fusion.123 = f32[8,16,3,3,3]{1,0,4,3,2:T(8,128)S(1)} fusion(bf16[1,16,10,6,256]{1,0,4,3,2:T(2,128)(2,1)} %copy.395, bf16[1,8,8,4,256]{1,0,4,3,2:T(2,128)(2,1)} %copy.396), kind=kOutput, calls=%fused_computation.182 | convolution fusion | flops 56475648 | bytes 636416 | tf_op jit(solution)/shard_map/transpose | solution.py:92
  593.8 27.9 %all-reduce.1 = (f32[16,8,3,3,3]{0,1,4,3,2:T(8,128)S(1)}, f32[8,16,3,3,3]{1,0,4,3,2:T(8,128)S(1)}) all-reduce(f32[16,8,3,3,3]{0,1,4,3,2:T(8,128)S(1)} %copy-done.11, f32[8,16,3,3,3]{1,0,4,3,2:T(8,128)S(1)} %fusion.123), channel_id=1, replica_groups=mesh['gy'=32,'gz'=8] {'gz'}, use_global_device_ids=true, to_apply=%region_0.1 | all-reduce | flops 6912 | bytes 55296 | tf_op jit(solution)/shard_map/psum | solution.py:123
  621.7 198.9 %all-reduce = (f32[16,8,3,3,3]{0,1,4,3,2:T(8,128)S(1)}, f32[8,16,3,3,3]{1,0,4,3,2:T(8,128)S(1)}) all-reduce(f32[16,8,3,3,3]{0,1,4,3,2:T(8,128)S(1)} %get-tuple-element.5, f32[8,16,3,3,3]{1,0,4,3,2:T(8,128)S(1)} %get-tuple-element.6), channel_id=1, replica_groups=mesh['gy'=32,'gz'=8] {'gy'}, use_global_device_ids=true, to_apply=%region_1.2 | all-reduce | flops 6912 | bytes 55296 | tf_op jit(solution)/shard_map/psum | solution.py:123
  826.9 9.3 %reshape.447 = bf16[8,2,4096]{2,1,0:T(2,128)(2,1)} reshape(bf16[8192,1,2,4]{3,2,1,0:T(2,128)(2,1)} %bitcast.304) | data formatting | bytes 262144
  836.2 34.9 %all-to-all-start.11 = ((bf16[8,2,4096]{2,1,0:T(2,128)(2,1)}), bf16[8,2,4096]{2,1,0:T(2,128)(2,1)S(1)}, u32[]{:S(2)}, u32[]{:S(2)}) async-start(bf16[8,2,4096]{2,1,0:T(2,128)(2,1)} %reshape.447), calls=%async_computation.11 | async-start | bytes 262144 | tf_op jit(solution)/shard_map/all_to_all | solution.py:62
  876.9 10.0 %reshape.448 = bf16[8192,1,2,4]{3,2,1,0:T(2,128)(2,1)} reshape(bf16[8,2,4096]{2,1,0:T(2,128)(2,1)S(1)} %all-to-all-done.11) | data formatting | bytes 262144
  886.9 9.6 %copy.381 = f32[2,4,8,4,256]{4,3,2,1,0:T(4,128)S(1)} copy(bf16[2,4,8,4,256]{1,0,4,3,2:T(2,128)(2,1)} %bitcast.305) | data formatting | bytes 393216 | tf_op jit(solution)/shard_map/convert_element_type | solution.py:64
  (213 shorter events, 297.4 us)
Async XLA Ops:
  12.0 26.5 %all-to-all-start.4 = ((f32[32,1,2048]{2,1,0:T(1,128)}), f32[32,1,2048]{2,1,0:T(1,128)S(1)}, u32[]{:S(2)}, u32[]{:S(2)}) async-start(f32[32,1,2048]{2,1,0:T(1,128)} %reshape.431), calls=%async_computation.4 | async-start | bytes 524288 | tf_op jit(solution)/shard_map/all_to_all | solution.py:47
  38.5 29.8 %all-to-all-start = ((f32[32,1,2048]{2,1,0:T(1,128)}), f32[32,1,2048]{2,1,0:T(1,128)S(1)}, u32[]{:S(2)}, u32[]{:S(2)}) async-start(f32[32,1,2048]{2,1,0:T(1,128)} %reshape.437), calls=%async_computation | async-start | bytes 524288 | tf_op jit(solution)/shard_map/all_to_all | solution.py:47
  68.3 27.0 %all-to-all-start.5 = ((f32[32,1,2048]{2,1,0:T(1,128)}), f32[32,1,2048]{2,1,0:T(1,128)S(1)}, u32[]{:S(2)}, u32[]{:S(2)}) async-start(f32[32,1,2048]{2,1,0:T(1,128)} %reshape.433), calls=%async_computation.5 | async-start | bytes 524288 | tf_op jit(solution)/shard_map/all_to_all | solution.py:51
  95.3 23.8 %all-to-all-start.1 = ((f32[32,1,2048]{2,1,0:T(1,128)}), f32[32,1,2048]{2,1,0:T(1,128)S(1)}, u32[]{:S(2)}, u32[]{:S(2)}) async-start(f32[32,1,2048]{2,1,0:T(1,128)} %reshape.439), calls=%async_computation.1 | async-start | bytes 524288 | tf_op jit(solution)/shard_map/all_to_all | solution.py:51
  119.1 16.2 %all-to-all-start.6 = ((f32[2,4,8,1024]{3,1,0,2:T(4,128)}), f32[2,4,8,1024]{3,1,0,2:T(4,128)S(1)}, u32[]{:S(2)}, u32[]{:S(2)}) async-start(f32[2,4,8,1024]{3,1,0,2:T(4,128)} %reshape.424), calls=%async_computation.6 | async-start | bytes 524288 | tf_op jit(solution)/shard_map/all_to_all | solution.py:50
  135.2 20.5 %all-to-all-start.2 = ((f32[2,4,8,1024]{3,1,0,2:T(4,128)}), f32[2,4,8,1024]{3,1,0,2:T(4,128)S(1)}, u32[]{:S(2)}, u32[]{:S(2)}) async-start(f32[2,4,8,1024]{3,1,0,2:T(4,128)} %reshape.422), calls=%async_computation.2 | async-start | bytes 524288 | tf_op jit(solution)/shard_map/all_to_all | solution.py:50
  155.8 20.7 %all-to-all-start.7 = ((bf16[8,2,4096]{2,1,0:T(2,128)(2,1)}), bf16[8,2,4096]{2,1,0:T(2,128)(2,1)S(1)}, u32[]{:S(2)}, u32[]{:S(2)}) async-start(bf16[8,2,4096]{2,1,0:T(2,128)(2,1)} %reshape.435), calls=%async_computation.7 | async-start | bytes 262144 | tf_op jit(solution)/shard_map/all_to_all | solution.py:62
  176.5 26.5 %all-to-all-start.3 = ((bf16[8,2,4096]{2,1,0:T(2,128)(2,1)}), bf16[8,2,4096]{2,1,0:T(2,128)(2,1)S(1)}, u32[]{:S(2)}, u32[]{:S(2)}) async-start(bf16[8,2,4096]{2,1,0:T(2,128)(2,1)} %reshape.441), calls=%async_computation.3 | async-start | bytes 262144 | tf_op jit(solution)/shard_map/all_to_all | solution.py:62
  201.1 34.8 %collective-permute-start.4 = (bf16[1,8,1,4,256]{4,3,2,1,0:T(4,128)(2,1)S(1)}, bf16[1,8,1,4,256]{4,3,2,1,0:T(4,128)(2,1)S(1)}, u32[]{:S(2)}, u32[]{:S(2)}) collective-permute-start(bf16[1,8,1,4,256]{4,3,2,1,0:T(4,128)(2,1)S(1)} %get-tuple-element.32), channel_id=1, source_target_pairs={{0,8},{8,16},{16,24},{24,32},{32,40},{40,48},{48,56},{56,64},{64,7... | collective-permute-start | bytes 49160 | tf_op jit(solution)/shard_map/ppermute | solution.py:19
  230.6 11.9 %collective-permute-start = (bf16[1,8,1,4,256]{4,3,2,1,0:T(4,128)(2,1)S(1)}, bf16[1,8,1,4,256]{4,3,2,1,0:T(4,128)(2,1)S(1)}, u32[]{:S(2)}, u32[]{:S(2)}) collective-permute-start(bf16[1,8,1,4,256]{4,3,2,1,0:T(4,128)(2,1)S(1)} %get-tuple-element.30), channel_id=1, source_target_pairs={{0,8},{8,16},{16,24},{24,32},{32,40},{40,48},{48,56},{56,64},{64,7... | collective-permute-start | bytes 49160 | tf_op jit(solution)/shard_map/ppermute | solution.py:19
  236.1 12.8 %collective-permute-start.6 = (bf16[1,8,10,1,256]{4,3,2,1,0:T(2,128)(2,1)S(1)}, bf16[1,8,10,1,256]{4,3,2,1,0:T(2,128)(2,1)S(1)}, u32[]{:S(2)}, u32[]{:S(2)}) collective-permute-start(bf16[1,8,10,1,256]{4,3,2,1,0:T(2,128)(2,1)S(1)} %get-tuple-element.27), channel_id=1, source_target_pairs={{0,1},{1,2},{2,3},{3,4},{4,5},{5,6},{6,7},{8,9},{9,10},{10,11},{11... | collective-permute-start | bytes 122888 | tf_op jit(solution)/shard_map/ppermute | solution.py:19
  243.3 17.3 %collective-permute-start.2 = (bf16[1,8,10,1,256]{4,3,2,1,0:T(2,128)(2,1)}, bf16[1,8,10,1,256]{4,3,2,1,0:T(2,128)(2,1)}, u32[]{:S(2)}, u32[]{:S(2)}) collective-permute-start(bf16[1,8,10,1,256]{4,3,2,1,0:T(2,128)(2,1)} %get-tuple-element.25), channel_id=1, source_target_pairs={{0,1},{1,2},{2,3},{3,4},{4,5},{5,6},{6,7},{8,9},{9,10},{10,11},{11... | collective-permute-start | bytes 122888 | tf_op jit(solution)/shard_map/ppermute | solution.py:19
  247.0 13.7 %collective-permute-start.3 = (bf16[1,8,10,1,256]{4,3,2,1,0:T(2,128)(2,1)}, bf16[1,8,10,1,256]{4,3,2,1,0:T(2,128)(2,1)}, u32[]{:S(2)}, u32[]{:S(2)}) collective-permute-start(bf16[1,8,10,1,256]{4,3,2,1,0:T(2,128)(2,1)} %get-tuple-element.26), channel_id=1, source_target_pairs={{1,0},{2,1},{3,2},{4,3},{5,4},{6,5},{7,6},{9,8},{10,9},{11,10},{12... | collective-permute-start | bytes 122888 | tf_op jit(solution)/shard_map/ppermute | solution.py:20
  296.5 122.4 %collective-permute-start.12 = (bf16[1,16,1,4,256]{4,1,3,0,2:T(8,128)(2,1)}, bf16[1,16,1,4,256]{4,1,3,0,2:T(8,128)(2,1)}, u32[]{:S(2)}, u32[]{:S(2)}) collective-permute-start(bf16[1,16,1,4,256]{4,1,3,0,2:T(8,128)(2,1)} %slice_bitcast_fusion.4), channel_id=1, source_target_pairs={{0,8},{8,16},{16,24},{24,32},{32,40},{40,48},{48,56},{56,64},{64,7... | collective-permute-start | bytes 98312 | tf_op jit(solution)/shard_map/ppermute | solution.py:19
  302.9 116.1 %collective-permute-start.13 = (bf16[1,16,1,4,256]{4,1,3,0,2:T(8,128)(2,1)}, bf16[1,16,1,4,256]{4,1,3,0,2:T(8,128)(2,1)}, u32[]{:S(2)}, u32[]{:S(2)}) collective-permute-start(bf16[1,16,1,4,256]{4,1,3,0,2:T(8,128)(2,1)} %slice_bitcast_fusion.3), channel_id=1, source_target_pairs={{8,0},{16,8},{24,16},{32,24},{40,32},{48,40},{56,48},{64,56},{72,6... | collective-permute-start | bytes 98312 | tf_op jit(solution)/shard_map/ppermute | solution.py:20
  306.4 13.5 %collective-permute-start.8 = (bf16[1,16,1,4,256]{4,1,3,0,2:T(8,128)(2,1)S(1)}, bf16[1,16,1,4,256]{4,1,3,0,2:T(8,128)(2,1)S(1)}, u32[]{:S(2)}, u32[]{:S(2)}) collective-permute-start(bf16[1,16,1,4,256]{4,1,3,0,2:T(8,128)(2,1)S(1)} %slice_bitcast_fusion.6), channel_id=1, source_target_pairs={{0,8},{8,16},{16,24},{24,32},{32,40},{40,48},{48,56},{56,64},{64,7... | collective-permute-start | bytes 98312 | tf_op jit(solution)/shard_map/ppermute | solution.py:19
  319.9 16.9 %collective-permute-start.10 = (bf16[1,16,10,1,256]{4,1,3,2,0:T(8,128)(2,1)S(1)}, bf16[1,16,10,1,256]{4,1,3,2,0:T(8,128)(2,1)S(1)}, u32[]{:S(2)}, u32[]{:S(2)}) collective-permute-start(bf16[1,16,10,1,256]{4,1,3,2,0:T(8,128)(2,1)S(1)} %get-tuple-element.19), channel_id=1, source_target_pairs={{0,1},{1,2},{2,3},{3,4},{4,5},{5,6},{6,7},{8,9},{9,10},{10,11},{11... | collective-permute-start | bytes 245768 | tf_op jit(solution)/shard_map/ppermute | solution.py:19
  324.4 12.4 %collective-permute-start.11 = (bf16[1,16,10,1,256]{4,1,3,2,0:T(8,128)(2,1)S(1)}, bf16[1,16,10,1,256]{4,1,3,2,0:T(8,128)(2,1)}, u32[]{:S(2)}, u32[]{:S(2)}) collective-permute-start(bf16[1,16,10,1,256]{4,1,3,2,0:T(8,128)(2,1)S(1)} %get-tuple-element.20), channel_id=1, source_target_pairs={{1,0},{2,1},{3,2},{4,3},{5,4},{6,5},{7,6},{9,8},{10,9},{11,10},{12... | collective-permute-start | bytes 245768 | tf_op jit(solution)/shard_map/ppermute | solution.py:20
  368.1 58.1 %all-to-all-start.8 = ((f32[32,1,2048]{2,1,0:T(1,128)}), f32[32,1,2048]{2,1,0:T(1,128)S(1)}, u32[]{:S(2)}, u32[]{:S(2)}) async-start(f32[32,1,2048]{2,1,0:T(1,128)} %reshape.443), calls=%async_computation.8 | async-start | bytes 524288 | tf_op jit(solution)/shard_map/all_to_all | solution.py:47
  420.4 61.1 %collective-permute-start.14 = (bf16[1,16,10,1,256]{4,1,3,2,0:T(8,128)(2,1)}, bf16[1,16,10,1,256]{4,1,3,2,0:T(8,128)(2,1)}, u32[]{:S(2)}, u32[]{:S(2)}) collective-permute-start(bf16[1,16,10,1,256]{4,1,3,2,0:T(8,128)(2,1)} %get-tuple-element.15), channel_id=1, source_target_pairs={{0,1},{1,2},{2,3},{3,4},{4,5},{5,6},{6,7},{8,9},{9,10},{10,11},{11... | collective-permute-start | bytes 245768 | tf_op jit(solution)/shard_map/ppermute | solution.py:19
  424.3 57.2 %collective-permute-start.15 = (bf16[1,16,10,1,256]{4,1,3,2,0:T(8,128)(2,1)}, bf16[1,16,10,1,256]{4,1,3,2,0:T(8,128)(2,1)}, u32[]{:S(2)}, u32[]{:S(2)}) collective-permute-start(bf16[1,16,10,1,256]{4,1,3,2,0:T(8,128)(2,1)} %get-tuple-element.16), channel_id=1, source_target_pairs={{1,0},{2,1},{3,2},{4,3},{5,4},{6,5},{7,6},{9,8},{10,9},{11,10},{12... | collective-permute-start | bytes 245768 | tf_op jit(solution)/shard_map/ppermute | solution.py:20
  446.3 48.2 %all-to-all-start.9 = ((f32[32,1,2048]{2,1,0:T(1,128)}), f32[32,1,2048]{2,1,0:T(1,128)S(1)}, u32[]{:S(2)}, u32[]{:S(2)}) async-start(f32[32,1,2048]{2,1,0:T(1,128)} %reshape.445), calls=%async_computation.9 | async-start | bytes 524288 | tf_op jit(solution)/shard_map/all_to_all | solution.py:51
  498.2 323.0 %all-to-all-start.10 = ((f32[2,4,8,1024]{3,1,0,2:T(4,128)}), f32[2,4,8,1024]{3,1,0,2:T(4,128)S(1)}, u32[]{:S(2)}, u32[]{:S(2)}) async-start(f32[2,4,8,1024]{3,1,0,2:T(4,128)} %reshape.426), calls=%async_computation.10 | async-start | bytes 524288 | tf_op jit(solution)/shard_map/all_to_all | solution.py:50
  836.2 40.7 %all-to-all-start.11 = ((bf16[8,2,4096]{2,1,0:T(2,128)(2,1)}), bf16[8,2,4096]{2,1,0:T(2,128)(2,1)S(1)}, u32[]{:S(2)}, u32[]{:S(2)}) async-start(bf16[8,2,4096]{2,1,0:T(2,128)(2,1)} %reshape.447), calls=%async_computation.11 | async-start | bytes 262144 | tf_op jit(solution)/shard_map/all_to_all | solution.py:62
  (20 other events, 1220.3 us)
